TPU v7x, 32 devices: a whole 2x2x4 slice. The times are simulated.
32 devices in a mesh: store: 8 (over y, x, core), dept: 4 (over z).
Axes of the slice: x: 2, y: 2, z: 4, core: 2. Of those that a mesh axis runs over, the one named last changes fastest.
Arguments:
- history: bfloat16 [2048, 96, 512], P('store', 'dept'), may hold values from -400 to 400, as said below
- input_layer_matrix: bfloat16 [512, 512], replicated, may hold values from -0.375 to 0.375
- middle_layer_matrix: bfloat16 [512, 512], replicated, may hold values from -0.375 to 0.375
- final_layer_matrix: bfloat16 [512, 28], replicated, may hold values from -0.375 to 0.375
Outputs:
- reconciled: float32 [2048, 2688], P('store', 'dept')
- store_gap: float32 [28, 2048], P(None, 'store')
- item_gap: float32 [28, 96], P(None, 'dept')
Inputs may be any that keep to these rules, and one draw needn't show every extreme that they name: `history`: daily sales histories.
All inputs are finite; a program needn't handle non-finite values.
Results may differ from a plain program's by a relative error of at most 0.0065.
The roundings to bfloat16 on the way count: a program that leaves them out, or rounds other values in their place, can miss the bound.
Values sent between devices are 32-bit elements; how exact they have to be, the bound alone decides.
A program may use at most 64 MiB of HBM per device.

v0:
```python
import functools
import math

import jax
import jax.numpy as jnp
from jax import lax
from jax.experimental import pallas as pl
from jax.experimental.pallas import tpu as pltpu
from jax.sharding import PartitionSpec as P

MESH = pl.DeviceIdType.MESH
F32 = jnp.float32
BF16 = jnp.bfloat16
SLOT = 32
PACK = 4
STORES_IN_CHUNK = 32
SCALED_ROWS = 128


def scales(values):
    mean = jnp.sum(values * values, axis=-1, keepdims=True) * (1.0 / values.shape[-1])
    return jnp.sqrt(mean + 1e-05)


def layers(blocks, w1, w2, w3):
    for weights in (w1, w2):
        blocks = [jnp.dot(block, weights[...], preferred_element_type=F32).astype(BF16) for block in blocks]
        blocks = [jnp.maximum(block, 0) for block in blocks]
    return [jnp.dot(block, w3[...], preferred_element_type=F32) for block in blocks]


def main_kernel(
    n_store, n_dept, stores, items, horizon,
    hist_hbm, w1_hbm, w2_hbm, w3_hbm,
    base_out, small_out,
    base, small, hist, scaled, w1, w2, w3_narrow, w3_wide, w3, selector, store_sums, store_recv, item_acc, item_sums, item_recv,
    sum_rows, flat, cs, cs_recv, up, up_recv, ci, ci_recv, err, err_recv,
    hist_sem, weight_sem, ss_send, ss_get, is_send, is_get, cs_send, cs_get, up_send, up_get,
    ci_send, ci_get, err_send, err_get, out_sem,
):
    my_store = lax.axis_index("store")
    my_dept = lax.axis_index("dept")
    own = stores // n_dept
    own_rows = own * items
    days = hist.shape[1]
    item_share = item_sums.shape[1]
    groups = -(-items // PACK)
    dept_order = sorted(range(1, n_dept), key=lambda o: -min(o, n_dept - o)) + [0]

    def dept_at(off):
        return lax.rem(my_dept + off, n_dept)

    def store_at(off):
        return lax.rem(my_store + off, n_store)

    def rows_of(chunk):
        return pl.ds(pl.multiple_of(chunk * own_rows, own_rows), own_rows)

    def load_chunk(off):
        rows = rows_of(dept_at(off))
        return pltpu.make_async_copy(hist_hbm.at[rows], hist.at[rows], hist_sem.at[off])

    for off in dept_order:
        load_chunk(off).start()
    load_w1 = pltpu.make_async_copy(w1_hbm, w1, weight_sem.at[0])
    load_w2 = pltpu.make_async_copy(w2_hbm, w2, weight_sem.at[1])
    load_w3 = pltpu.make_async_copy(w3_hbm, w3_narrow, weight_sem.at[2])
    load_w3.start()
    load_w1.start()
    load_w2.start()

    barrier = pltpu.get_barrier_semaphore()

    for off in range(1, n_dept):
        pl.semaphore_signal(barrier, inc=1, device_id=(my_store, dept_at(off)), device_id_type=MESH)
    for off in range(1, n_store):
        pl.semaphore_signal(barrier, inc=1, device_id=(store_at(off), my_dept), device_id_type=MESH)

    row = lax.broadcasted_iota(jnp.int32, selector.shape, 0)
    col = lax.broadcasted_iota(jnp.int32, selector.shape, 1)
    of_store = (col >= row * items) & (col < row * items + items)
    col_f = col.astype(F32)
    which = col_f - items * jnp.floor((col_f + 0.5) * (1.0 / items))
    of_item = which == (row - own).astype(F32)
    selector[...] = jnp.where(row < own, of_store.astype(F32), of_item.astype(F32)).astype(BF16)

    w3_wide[...] = jnp.zeros_like(w3_wide)
    load_w3.wait()
    last_layer = w3_narrow[...].astype(F32)
    for j in range(PACK):
        w3_wide[j * SLOT:j * SLOT + horizon, :] = last_layer
    w3[...] = w3_wide[...].T.astype(BF16)

    pl.semaphore_wait(barrier, n_dept + n_store - 2)

    def send_store(off):
        return pltpu.make_async_remote_copy(
            src_ref=store_sums.at[dept_at(off)], dst_ref=store_recv.at[off],
            send_sem=ss_send.at[off], recv_sem=ss_get.at[off],
            device_id=(my_store, dept_at(off)), device_id_type=MESH,
        )

    def send_item(off):
        return pltpu.make_async_remote_copy(
            src_ref=item_sums.at[store_at(off)], dst_ref=item_recv.at[off],
            send_sem=is_send.at[off], recv_sem=is_get.at[off],
            device_id=(store_at(off), my_dept), device_id_type=MESH,
        )

    item_total = None
    for off in dept_order:
        load_chunk(off).wait()
        sums = jnp.dot(selector[...], hist[rows_of(dept_at(off)), :], preferred_element_type=F32)
        store_sums[dept_at(off)] = sums[:own]
        if off:
            send_store(off).start()
        item_total = sums[own:] if item_total is None else item_total + sums[own:]
    item_acc[...] = jnp.zeros_like(item_acc)
    item_acc[0:items, :] = item_total
    for place in range(n_store):
        item_sums[place] = item_acc[place * item_share:(place + 1) * item_share, :]
    for off in range(1, n_store):
        send_item(off).start()

    load_w1.wait()
    load_w2.wait()
    half = 128
    lane = lax.broadcasted_iota(jnp.int32, (half, 128), 1)
    col_parts = [None] * groups

    def send_cs(off, part):
        return pltpu.make_async_remote_copy(
            src_ref=cs.at[part], dst_ref=cs_recv.at[off, part],
            send_sem=cs_send.at[off, part], recv_sem=cs_get.at[off, part],
            device_id=(my_store, dept_at(off)), device_id_type=MESH,
        )

    def send_up(off):
        return pltpu.make_async_remote_copy(
            src_ref=up, dst_ref=up_recv.at[off], send_sem=up_send.at[off], recv_sem=up_get.at[off],
            device_id=(my_store, dept_at(off)), device_id_type=MESH,
        )

    def scale(first, count):
        for start in range(first, first + count, SCALED_ROWS):
            rows = slice(start, start + SCALED_ROWS)
            root_mean = scales(hist[rows, :].astype(F32))
            flat[rows, :] = jnp.broadcast_to(root_mean, (SCALED_ROWS, 128))
            scaled[rows, :] = (hist[rows, :].astype(F32) * (1.0 / root_mean)).astype(BF16)

    def run(first, sizes, more=()):
        starts = [first + sum(sizes[:i]) for i in range(len(sizes))]
        pieces = [slice(start, start + size) for start, size in zip(starts, sizes)]
        results = layers(list(more) + [scaled[rows, :] for rows in pieces], w1, w2, w3)
        for rows, result in zip(pieces, results[len(more):]):
            flat[rows, :] = result * flat[rows, :]
        return results[:len(more)]

    def turn(part):
        row_part = None
        for k in range(groups):
            mixed = jnp.zeros((half, 128), F32)
            for j in range(PACK):
                if k * PACK + j < items:
                    one = flat[pl.ds(part * half * items + k * PACK + j, half, stride=items), :]
                    mixed = jnp.where((lane >= j * SLOT) & (lane < (j + 1) * SLOT), one, mixed)
            col_sum = jnp.sum(mixed, axis=0, keepdims=True)
            col_parts[k] = col_sum if col_parts[k] is None else col_parts[k] + col_sum
            turned = mixed.T
            base[k * 128:(k + 1) * 128, part * half:(part + 1) * half] = turned
            row_part = turned if row_part is None else row_part + turned
        cs[part] = sum(row_part[j * SLOT:(j + 1) * SLOT] for j in range(PACK))
        for off in dept_order[:-1]:
            send_cs(off, part).start()

    block = STORES_IN_CHUNK * items
    blocks = stores // STORES_IN_CHUNK
    blocks_in_half = half // STORES_IN_CHUNK
    scale(0, 2 * block)
    for number in range(0, blocks - 2, 2):
        run(number * block, [block, block])
        scale((number + 2) * block, 2 * block)
        if (number + 2) % blocks_in_half == 0:
            turn((number + 2) // blocks_in_half - 1)

    sum_rows[own:, :] = jnp.zeros((sum_rows.shape[0] - own, days), F32)
    store_total = store_sums[my_dept]
    for off in range(1, n_dept):
        send_store(off).wait_recv()
        store_total = store_total + store_recv[off]
    sum_rows[0:own, :] = store_total
    item_total = item_sums[my_store]
    for off in range(1, n_store):
        send_item(off).wait_recv()
        item_total = item_total + item_recv[off]
    sum_rows[own:own + item_share, :] = item_total
    upper_mean = scales(sum_rows[...])
    upper_scaled = (sum_rows[...] * (1.0 / upper_mean)).astype(BF16)
    (upper,) = run((blocks - 2) * block, [block], [upper_scaled])
    upper = upper * upper_mean
    up[...] = jnp.concatenate([upper[:own]] * (128 // own), axis=0).T[:SLOT]
    for off in dept_order[:-1]:
        send_up(off).start()

    run((blocks - 1) * block, [block // 2, block // 2])
    turn(stores // half - 1)
    write_base = pltpu.make_async_copy(base, base_out, out_sem.at[0])
    write_base.start()

    packed = lax.broadcasted_iota(jnp.int32, ci.shape, 0) * PACK
    packed_lane = lax.broadcasted_iota(jnp.int32, ci.shape, 1)
    for j in range(1, PACK):
        packed = packed + (packed_lane >= j * SLOT).astype(jnp.int32)
    ci[...] = jnp.zeros_like(ci)
    for k in range(groups):
        ci[k:k + 1, :] = 0.0 - col_parts[k]
    ci_mine = ci[...]
    for t in range(item_share):
        number = my_store * item_share + t
        ci_mine = ci_mine + jnp.where((packed == number) & (packed < items), upper[own + t:own + t + 1], 0.0)
    base_total = sum(col_parts)
    base_total = base_total + pltpu.roll(base_total, 2 * SLOT, 1)
    base_total = base_total + pltpu.roll(base_total, SLOT, 1)
    ci[...] = ci_mine
    ci[groups:groups + 1, :] = jnp.sum(upper[:own], axis=0, keepdims=True) - base_total
    ci[groups + 1:groups + 2, :] = jnp.sum(upper[own:own + item_share], axis=0, keepdims=True) - base_total

    def send_ci(off):
        return pltpu.make_async_remote_copy(
            src_ref=ci, dst_ref=ci_recv.at[off], send_sem=ci_send.at[off], recv_sem=ci_get.at[off],
            device_id=(store_at(off), my_dept), device_id_type=MESH,
        )

    def send_err(off):
        return pltpu.make_async_remote_copy(
            src_ref=err, dst_ref=err_recv.at[off], send_sem=err_send.at[off], recv_sem=err_get.at[off],
            device_id=(my_store, dept_at(off)), device_id_type=MESH,
        )

    for off in range(1, n_store):
        send_ci(off).start()

    item_err = ci[...]
    for off in range(1, n_store):
        send_ci(off).wait_recv()
        item_err = item_err + ci_recv[off]

    err[...] = item_err[groups:groups + 2]
    for off in range(1, n_dept):
        send_err(off).start()

    place = lax.broadcasted_iota(jnp.int32, (SLOT, stores), 1)

    def placed(piece, owner):
        mine = (place >= owner * own) & (place < (owner + 1) * own)
        return jnp.where(mine, jnp.concatenate([piece] * (stores // 128), axis=1), 0.0)

    store_parts = [cs[part] for part in range(stores // half)]
    store_err = placed(up[...], my_dept)
    for off in range(1, n_dept):
        for part in range(stores // half):
            send_cs(off, part).wait_recv()
            store_parts[part] = store_parts[part] + cs_recv[off, part]
        send_up(off).wait_recv()
        store_err = store_err + placed(up_recv[off], dept_at(n_dept - off))
    store_err = store_err - jnp.concatenate(store_parts, axis=1)
    errs = err[...]
    for off in range(1, n_dept):
        send_err(off).wait_recv()
        errs = errs + err_recv[off]
    err_s, err_i = errs[0:1], errs[1:2]
    item_count = float(items * n_dept)
    store_count = float(stores * n_store)
    denominator = 1.0 + item_count + store_count
    shift_s = (err_s * (1.0 + store_count) - store_count * err_i) / denominator
    shift_i = ((1.0 + item_count) * err_i - item_count * err_s) / denominator
    shift_i_col = jnp.broadcast_to(shift_i, (128, 128)).T[:SLOT]
    shift_i_all = jnp.concatenate([shift_i_col] * (stores // 128), axis=1)
    small[0:SLOT, :] = (store_err - shift_i_all) * (1.0 / (1.0 + item_count))
    small[SLOT:2 * SLOT, :] = store_err * (1.0 / math.sqrt(item_count))
    small[2 * SLOT:, 0:128] = (item_err - shift_s) * (1.0 / (1.0 + store_count))
    small[2 * SLOT:, 128:256] = item_err * (1.0 / math.sqrt(store_count))
    write_small = pltpu.make_async_copy(small, small_out, out_sem.at[1])
    write_small.start()

    for off in range(1, n_dept):
        send_store(off).wait_send()
        send_up(off).wait_send()
        send_err(off).wait_send()
        for part in range(stores // half):
            send_cs(off, part).wait_send()
    for off in range(1, n_store):
        send_item(off).wait_send()
        send_ci(off).wait_send()
    write_base.wait()
    write_small.wait()


def final_kernel(
    items, horizon, base_hbm, small_hbm, reconciled_out, store_gap_out, item_gap_out,
    base, small, reconciled, store_gap, item_gap, read_sem, write_sem,
):
    groups = base.shape[0] // 128
    read_small = pltpu.make_async_copy(small_hbm, small, read_sem.at[groups])
    read_small.start()
    reads, writes = [], []
    for k in range(groups):
        rows = pl.ds(k * 128, 128)
        reads.append(pltpu.make_async_copy(base_hbm.at[rows], base.at[rows], read_sem.at[k]))
        reads[k].start()
    read_small.wait()
    shift = small[0:SLOT, :]
    item_shift = small[2 * SLOT:, 0:128]
    gap = small[2 * SLOT:, 128:256]
    columns = jnp.concatenate([item_shift] + [jnp.zeros((128 - item_shift.shape[0], 128), F32)], axis=0).T
    store_gap[...] = small[SLOT:SLOT + horizon, :]
    for item in range(items):
        k, j = divmod(item, PACK)
        item_gap[item:item + 1, :] = gap[k:k + 1, j * SLOT:j * SLOT + horizon]
    writes.append(pltpu.make_async_copy(store_gap, store_gap_out, write_sem.at[groups]))
    writes.append(pltpu.make_async_copy(item_gap, item_gap_out, write_sem.at[groups + 1]))
    writes[0].start()
    writes[1].start()
    for k in range(groups):
        reads[k].wait()
        mine = range(k * PACK, min((k + 1) * PACK, items))
        for item in mine:
            j = item - k * PACK
            first = k * 128 + j * SLOT
            block = base[first:first + SLOT, :] + shift + columns[j * SLOT:(j + 1) * SLOT, k:k + 1]
            reconciled[item * horizon:(item + 1) * horizon, :] = block[:horizon]
        rows = pl.ds(mine[0] * horizon, len(mine) * horizon)
        writes.append(pltpu.make_async_copy(reconciled.at[rows], reconciled_out.at[rows], write_sem.at[k]))
        writes[-1].start()
    for write in writes:
        write.wait()


def body(n_store, n_dept, history, input_layer_matrix, middle_layer_matrix, final_layer_matrix):
    stores, items, days = history.shape
    hidden = input_layer_matrix.shape[1]
    horizon = final_layer_matrix.shape[1]
    own = stores // n_dept
    item_share = -(-items // n_store)
    groups = -(-items // PACK)
    group_rows = -(-(groups + 2) // 8) * 8
    share_rows = -(-item_share // 8) * 8
    in_hbm = pl.BlockSpec(memory_space=pl.ANY)
    dma = pltpu.SemaphoreType.DMA
    shape = jax.ShapeDtypeStruct
    parts = pl.pallas_call(
        functools.partial(main_kernel, n_store, n_dept, stores, items, horizon),
        out_shape=(
            shape((groups * 128, stores), F32),
            shape((2 * SLOT + group_rows, stores), F32),
        ),
        in_specs=[in_hbm] * 4,
        out_specs=[in_hbm] * 2,
        scratch_shapes=[
            pltpu.VMEM((groups * 128, stores), F32),
            pltpu.VMEM((2 * SLOT + group_rows, stores), F32),
            pltpu.VMEM((stores * items, days), BF16),
            pltpu.VMEM((stores * items, days), BF16),
            pltpu.VMEM((days, hidden), BF16),
            pltpu.VMEM((hidden, hidden), BF16),
            pltpu.VMEM((horizon, hidden), BF16),
            pltpu.VMEM((128, hidden), F32),
            pltpu.VMEM((hidden, 128), BF16),
            pltpu.VMEM((own + items, own * items), BF16),
            pltpu.VMEM((n_dept, own, days), F32),
            pltpu.VMEM((n_dept, own, days), F32),
            pltpu.VMEM((-(-n_store * item_share // 8) * 8, days), F32),
            pltpu.VMEM((n_store, item_share, days), F32),
            pltpu.VMEM((n_store, item_share, days), F32),
            pltpu.VMEM((own + share_rows, days), F32),
            pltpu.VMEM((stores * items, 128), F32),
            pltpu.VMEM((stores // 128, SLOT, 128), F32),
            pltpu.VMEM((n_dept, stores // 128, SLOT, 128), F32),
            pltpu.VMEM((SLOT, 128), F32),
            pltpu.VMEM((n_dept, SLOT, 128), F32),
            pltpu.VMEM((group_rows, 128), F32),
            pltpu.VMEM((n_store, group_rows, 128), F32),
            pltpu.VMEM((2, 128), F32),
            pltpu.VMEM((n_dept, 2, 128), F32),
            dma((n_dept,)),
            dma((3,)),
            dma((n_dept,)),
            dma((n_dept,)),
            dma((n_store,)),
            dma((n_store,)),
            dma((n_dept, stores // 128)),
            dma((n_dept, stores // 128)),
            dma((n_dept,)),
            dma((n_dept,)),
            dma((n_store,)),
            dma((n_store,)),
            dma((n_dept,)),
            dma((n_dept,)),
            dma((2,)),
        ],
        compiler_params=pltpu.CompilerParams(
            collective_id=0, has_side_effects=True, vmem_limit_bytes=60 * 2**20
        ),
    )(
        history.reshape(stores * items, days),
        input_layer_matrix,
        middle_layer_matrix,
        final_layer_matrix.T,
    )
    reconciled, store_gap, item_gap = pl.pallas_call(
        functools.partial(final_kernel, items, horizon),
        out_shape=(
            shape((items * horizon, stores), F32),
            shape((horizon, stores), F32),
            shape((items, horizon), F32),
        ),
        in_specs=[in_hbm] * 2,
        out_specs=[in_hbm] * 3,
        scratch_shapes=[
            pltpu.VMEM((groups * 128, stores), F32),
            pltpu.VMEM((2 * SLOT + group_rows, stores), F32),
            pltpu.VMEM((items * horizon, stores), F32),
            pltpu.VMEM((horizon, stores), F32),
            pltpu.VMEM((items, horizon), F32),
            dma((groups + 1,)),
            dma((groups + 2,)),
        ],
        compiler_params=pltpu.CompilerParams(vmem_limit_bytes=60 * 2**20),
    )(*parts)
    return reconciled.T, store_gap, item_gap.T


def solution(mesh):
    return jax.shard_map(
        functools.partial(body, mesh.shape["store"], mesh.shape["dept"]),
        mesh=mesh,
        in_specs=(P("store", "dept", None), P(), P(), P()),
        out_specs=(P("store", "dept"), P(None, "store"), P(None, "dept")),
        check_vma=False,
    )
```

profile of v0, /device:TPU:0, one launch (start us, length us, event | category | flops | bytes accessed | tf_op | source)
XLA Modules:
  0.0 33.6 jit_solution(17910329970635766419)
XLA Ops:
  0.6 30.6 %shard_map.67 = (f32[768,256]{1,0:T(8,128)}, f32[72,256]{1,0:T(8,128)}) custom-call(bf16[6144,512]{1,0:T(8,128)(2,1)} %bitcast.4, bf16[512,512]{1,0:T(8,128)(2,1)} %w1_hbm.1, bf16[512,512]{1,0:T(8,128)(2,1)} %w2_hbm.1, bf16[28,512]{1,0:T(8,128)(2,1)} %bitcast.5), custom_call_target="tpu_custom_call" | custom-call | tf_op jit(solution)/shard_map/pallas_call | solution.py:351
  31.3 2.3 %shard_map.68 = (f32[672,256]{1,0:T(8,128)}, f32[28,256]{1,0:T(8,128)}, f32[24,28]{1,0:T(8,128)}) custom-call(f32[768,256]{1,0:T(8,128)} %get-tuple-element.8.base_hbm, f32[72,256]{1,0:T(8,128)} %get-tuple-element.9.small_hbm), custom_call_target="tpu_custom_call" | custom-call | tf_op jit(solution)/shard_map/pallas_call | solution.py:410
where the time goes:
time: 33.7 us; the launch traced here: 33.6 us
  Pallas kernels  33 us (98%)
  between operations  0.64 us (2%)
    pallas_call x1, Pallas kernels, body(): pl.pallas_call(functools.partial(main_kernel, n_store, n_dept, stores, it...  30.6 us
    pallas_call x1, Pallas kernels, body(): pl.pallas_call(functools.partial(final_kernel, items, horizon), out_shape...  2.31 us

commit v1 on v0

--- a/solution.py
+++ b/solution.py
@@ -33,9 +33,9 @@
     n_store, n_dept, stores, items, horizon,
     hist_hbm, w1_hbm, w2_hbm, w3_hbm,
     base_out, small_out,
-    base, small, hist, scaled, w1, w2, w3_narrow, w3_wide, w3, selector, store_sums, store_recv, item_acc, item_sums, item_recv,
+    base, small, hist, scaled, w1, w2, w3_narrow, w3_wide, w3, selector, store_sums, pair_recv, store_recv, item_acc, item_sums, item_recv,
     sum_rows, flat, cs, cs_recv, up, up_recv, ci, ci_recv, err, err_recv,
-    hist_sem, weight_sem, ss_send, ss_get, is_send, is_get, cs_send, cs_get, up_send, up_get,
+    hist_sem, weight_sem, sp_send, sp_get, ss_send, ss_get, is_send, is_get, cs_send, cs_get, up_send, up_get,
     ci_send, ci_get, err_send, err_get, out_sem,
 ):
     my_store = lax.axis_index("store")
@@ -56,12 +56,15 @@
     def rows_of(chunk):
         return pl.ds(pl.multiple_of(chunk * own_rows, own_rows), own_rows)
 
-    def load_chunk(off):
-        rows = rows_of(dept_at(off))
-        return pltpu.make_async_copy(hist_hbm.at[rows], hist.at[rows], hist_sem.at[off])
-
-    for off in dept_order:
-        load_chunk(off).start()
+    def load_chunk(slot, chunk):
+        rows = rows_of(chunk)
+        return pltpu.make_async_copy(hist_hbm.at[rows], hist.at[rows], hist_sem.at[slot])
+
+    early = lax.rem(my_dept + 1, 2) + my_dept - lax.rem(my_dept, 2)
+    for slot in range(n_dept):
+        near = slot % (n_dept // 2) == n_dept // 2 - 1
+        ahead = 0 if near else 2 * (slot % (n_dept // 2) + 1)
+        load_chunk(slot, lax.rem((early if slot < n_dept // 2 else my_dept) + ahead, n_dept)).start()
     load_w1 = pltpu.make_async_copy(w1_hbm, w1, weight_sem.at[0])
     load_w2 = pltpu.make_async_copy(w2_hbm, w2, weight_sem.at[1])
     load_w3 = pltpu.make_async_copy(w3_hbm, w3_narrow, weight_sem.at[2])
@@ -93,11 +96,24 @@
 
     pl.semaphore_wait(barrier, n_dept + n_store - 2)
 
-    def send_store(off):
-        return pltpu.make_async_remote_copy(
-            src_ref=store_sums.at[dept_at(off)], dst_ref=store_recv.at[off],
-            send_sem=ss_send.at[off], recv_sem=ss_get.at[off],
-            device_id=(my_store, dept_at(off)), device_id_type=MESH,
+    partner = my_dept + 1 - 2 * lax.rem(my_dept, 2)
+    pairs = n_dept // 2
+
+    def partner_block(m):
+        return lax.rem(partner + 2 * m, n_dept)
+
+    def send_pair(m):
+        return pltpu.make_async_remote_copy(
+            src_ref=store_sums.at[partner_block(m)], dst_ref=pair_recv.at[m],
+            send_sem=sp_send.at[m], recv_sem=sp_get.at[m],
+            device_id=(my_store, partner), device_id_type=MESH,
+        )
+
+    def send_store(m):
+        return pltpu.make_async_remote_copy(
+            src_ref=store_sums.at[dept_at(2 * m)], dst_ref=store_recv.at[m],
+            send_sem=ss_send.at[m], recv_sem=ss_get.at[m],
+            device_id=(my_store, dept_at(2 * m)), device_id_type=MESH,
         )
 
     def send_item(off):
@@ -108,12 +124,14 @@
         )
 
     item_total = None
-    for off in dept_order:
-        load_chunk(off).wait()
-        sums = jnp.dot(selector[...], hist[rows_of(dept_at(off)), :], preferred_element_type=F32)
-        store_sums[dept_at(off)] = sums[:own]
-        if off:
-            send_store(off).start()
+    far_first = list(range(1, pairs)) + [0]
+    for slot, (m, sent) in enumerate([(m, True) for m in far_first] + [(m, False) for m in far_first]):
+        chunk = partner_block(m) if sent else dept_at(2 * m)
+        load_chunk(slot, chunk).wait()
+        sums = jnp.dot(selector[...], hist[rows_of(chunk), :], preferred_element_type=F32)
+        store_sums[chunk] = sums[:own]
+        if sent:
+            send_pair(m).start()
         item_total = sums[own:] if item_total is None else item_total + sums[own:]
     item_acc[...] = jnp.zeros_like(item_acc)
     item_acc[0:items, :] = item_total
@@ -180,14 +198,22 @@
     for number in range(0, blocks - 2, 2):
         run(number * block, [block, block])
         scale((number + 2) * block, 2 * block)
+        if number == 0:
+            for m in range(1, pairs):
+                send_pair(m).wait_recv()
+                store_sums[dept_at(2 * m)] = store_sums[dept_at(2 * m)] + pair_recv[m]
+                send_store(m).start()
         if (number + 2) % blocks_in_half == 0:
             turn((number + 2) // blocks_in_half - 1)
 
+    run((blocks - 2) * block, [block // 2, block // 2])
+
     sum_rows[own:, :] = jnp.zeros((sum_rows.shape[0] - own, days), F32)
-    store_total = store_sums[my_dept]
-    for off in range(1, n_dept):
-        send_store(off).wait_recv()
-        store_total = store_total + store_recv[off]
+    send_pair(0).wait_recv()
+    store_total = store_sums[my_dept] + pair_recv[0]
+    for m in range(1, pairs):
+        send_store(m).wait_recv()
+        store_total = store_total + store_recv[m]
     sum_rows[0:own, :] = store_total
     item_total = item_sums[my_store]
     for off in range(1, n_store):
@@ -196,13 +222,12 @@
     sum_rows[own:own + item_share, :] = item_total
     upper_mean = scales(sum_rows[...])
     upper_scaled = (sum_rows[...] * (1.0 / upper_mean)).astype(BF16)
-    (upper,) = run((blocks - 2) * block, [block], [upper_scaled])
+    (upper,) = run((blocks - 1) * block, [block], [upper_scaled])
     upper = upper * upper_mean
     up[...] = jnp.concatenate([upper[:own]] * (128 // own), axis=0).T[:SLOT]
     for off in dept_order[:-1]:
         send_up(off).start()
 
-    run((blocks - 1) * block, [block // 2, block // 2])
     turn(stores // half - 1)
     write_base = pltpu.make_async_copy(base, base_out, out_sem.at[0])
     write_base.start()
@@ -284,11 +309,14 @@
     write_small.start()
 
     for off in range(1, n_dept):
-        send_store(off).wait_send()
         send_up(off).wait_send()
         send_err(off).wait_send()
         for part in range(stores // half):
             send_cs(off, part).wait_send()
+    for m in range(pairs):
+        send_pair(m).wait_send()
+        if m:
+            send_store(m).wait_send()
     for off in range(1, n_store):
         send_item(off).wait_send()
         send_ci(off).wait_send()
@@ -368,7 +396,8 @@
             pltpu.VMEM((hidden, 128), BF16),
             pltpu.VMEM((own + items, own * items), BF16),
             pltpu.VMEM((n_dept, own, days), F32),
-            pltpu.VMEM((n_dept, own, days), F32),
+            pltpu.VMEM((n_dept // 2, own, days), F32),
+            pltpu.VMEM((n_dept // 2, own, days), F32),
             pltpu.VMEM((-(-n_store * item_share // 8) * 8, days), F32),
             pltpu.VMEM((n_store, item_share, days), F32),
             pltpu.VMEM((n_store, item_share, days), F32),
@@ -384,8 +413,10 @@
             pltpu.VMEM((n_dept, 2, 128), F32),
             dma((n_dept,)),
             dma((3,)),
-            dma((n_dept,)),
-            dma((n_dept,)),
+            dma((n_dept // 2,)),
+            dma((n_dept // 2,)),
+            dma((n_dept // 2,)),
+            dma((n_dept // 2,)),
             dma((n_store,)),
             dma((n_store,)),
             dma((n_dept, stores // 128)),

time: 33.7 us -> 32.5 us (0.964)
  Pallas kernels: 33 us -> 31.7 us
    pallas_call x1, Pallas kernels: 30.6 us -> 29.4 us  [body(): pl.pallas_call(functools.partial(main_kernel, n_store, n_dept, stores, it...]
where the time goes in v1:
time: 32.5 us; the launch traced here: 32.4 us
  Pallas kernels  31.7 us (98%)
  between operations  0.64 us (2%)
    pallas_call x1, Pallas kernels, body(): pl.pallas_call(functools.partial(main_kernel, n_store, n_dept, stores, it...  29.4 us
    pallas_call x1, Pallas kernels, body(): pl.pallas_call(functools.partial(final_kernel, items, horizon), out_shape...  2.31 us

profile of v1, /device:TPU:0, one launch (start us, length us, event | category | flops | bytes accessed | tf_op | source)
XLA Modules:
  0.0 32.4 jit_solution(5129370193591152582)
XLA Ops:
  0.6 29.4 %shard_map.67 = (f32[768,256]{1,0:T(8,128)}, f32[72,256]{1,0:T(8,128)}) custom-call(bf16[6144,512]{1,0:T(8,128)(2,1)} %bitcast.4, bf16[512,512]{1,0:T(8,128)(2,1)} %w1_hbm.1, bf16[512,512]{1,0:T(8,128)(2,1)} %w2_hbm.1, bf16[28,512]{1,0:T(8,128)(2,1)} %bitcast.5), custom_call_target="tpu_custom_call" | custom-call | tf_op jit(solution)/shard_map/pallas_call | solution.py:379
  30.1 2.3 %shard_map.68 = (f32[672,256]{1,0:T(8,128)}, f32[28,256]{1,0:T(8,128)}, f32[24,28]{1,0:T(8,128)}) custom-call(f32[768,256]{1,0:T(8,128)} %get-tuple-element.8.base_hbm, f32[72,256]{1,0:T(8,128)} %get-tuple-element.9.small_hbm), custom_call_target="tpu_custom_call" | custom-call | tf_op jit(solution)/shard_map/pallas_call | solution.py:441

commit v2 on v1

--- a/solution.py
+++ b/solution.py
@@ -160,11 +160,16 @@
         )
 
     def scale(first, count):
-        for start in range(first, first + count, SCALED_ROWS):
-            rows = slice(start, start + SCALED_ROWS)
-            root_mean = scales(hist[rows, :].astype(F32))
-            flat[rows, :] = jnp.broadcast_to(root_mean, (SCALED_ROWS, 128))
-            scaled[rows, :] = (hist[rows, :].astype(F32) * (1.0 / root_mean)).astype(BF16)
+        def step(i, carry):
+            for part in range(3):
+                start = first + (i * 3 + part) * SCALED_ROWS
+                rows = pl.ds(pl.multiple_of(start, SCALED_ROWS), SCALED_ROWS)
+                root_mean = scales(hist[rows, :].astype(F32))
+                flat[rows, :] = jnp.broadcast_to(root_mean, (SCALED_ROWS, 128))
+                scaled[rows, :] = (hist[rows, :].astype(F32) * (1.0 / root_mean)).astype(BF16)
+            return carry
+
+        lax.fori_loop(0, count // (3 * SCALED_ROWS), step, 0)
 
     def run(first, sizes, more=()):
         starts = [first + sum(sizes[:i]) for i in range(len(sizes))]
@@ -196,7 +201,14 @@
     blocks_in_half = half // STORES_IN_CHUNK
     scale(0, 2 * block)
     for number in range(0, blocks - 2, 2):
-        run(number * block, [block, block])
+        def step(i, carry, number=number):
+            starts = [(number + i) * block + part * (block // 2) for part in range(2)]
+            pieces = [pl.ds(pl.multiple_of(start, SCALED_ROWS), block // 2) for start in starts]
+            for rows, result in zip(pieces, layers([scaled[rows, :] for rows in pieces], w1, w2, w3)):
+                flat[rows, :] = result * flat[rows, :]
+            return carry
+
+        lax.fori_loop(0, 2, step, 0)
         scale((number + 2) * block, 2 * block)
         if number == 0:
             for m in range(1, pairs):

time: 32.5 us -> 32.9 us (1.012)
  Pallas kernels: 31.7 us -> 32.1 us
    pallas_call x1, Pallas kernels: 29.4 us -> 29.8 us  [body(): pl.pallas_call(functools.partial(main_kernel, n_store, n_dept, stores, it...]
where the time goes in v2:
time: 32.9 us; the launch traced here: 32.8 us
  Pallas kernels  32.1 us (98%)
  between operations  0.64 us (2%)
    pallas_call x1, Pallas kernels, body(): pl.pallas_call(functools.partial(main_kernel, n_store, n_dept, stores, it...  29.8 us
    pallas_call x1, Pallas kernels, body(): pl.pallas_call(functools.partial(final_kernel, items, horizon), out_shape...  2.31 us

profile of v2, /device:TPU:0, one launch (start us, length us, event | category | flops | bytes accessed | tf_op | source)
XLA Modules:
  0.0 32.8 jit_solution(2065129119425539036)
XLA Ops:
  0.6 29.8 %shard_map.67 = (f32[768,256]{1,0:T(8,128)}, f32[72,256]{1,0:T(8,128)}) custom-call(bf16[6144,512]{1,0:T(8,128)(2,1)} %bitcast.4, bf16[512,512]{1,0:T(8,128)(2,1)} %w1_hbm.1, bf16[512,512]{1,0:T(8,128)(2,1)} %w2_hbm.1, bf16[28,512]{1,0:T(8,128)(2,1)} %bitcast.5), custom_call_target="tpu_custom_call" | custom-call | tf_op jit(solution)/shard_map/pallas_call | solution.py:391
  30.5 2.3 %shard_map.68 = (f32[672,256]{1,0:T(8,128)}, f32[28,256]{1,0:T(8,128)}, f32[24,28]{1,0:T(8,128)}) custom-call(f32[768,256]{1,0:T(8,128)} %get-tuple-element.8.base_hbm, f32[72,256]{1,0:T(8,128)} %get-tuple-element.9.small_hbm), custom_call_target="tpu_custom_call" | custom-call | tf_op jit(solution)/shard_map/pallas_call | solution.py:453

commit v3 on v1

--- a/solution.py
+++ b/solution.py
@@ -206,7 +206,10 @@
         if (number + 2) % blocks_in_half == 0:
             turn((number + 2) // blocks_in_half - 1)
 
-    run((blocks - 2) * block, [block // 2, block // 2])
+    run((blocks - 2) * block, [block, block])
+    turn(stores // half - 1)
+    write_base = pltpu.make_async_copy(base, base_out, out_sem.at[0])
+    write_base.start()
 
     sum_rows[own:, :] = jnp.zeros((sum_rows.shape[0] - own, days), F32)
     send_pair(0).wait_recv()
@@ -222,15 +225,12 @@
     sum_rows[own:own + item_share, :] = item_total
     upper_mean = scales(sum_rows[...])
     upper_scaled = (sum_rows[...] * (1.0 / upper_mean)).astype(BF16)
-    (upper,) = run((blocks - 1) * block, [block], [upper_scaled])
+    (upper,) = layers([upper_scaled], w1, w2, w3)
     upper = upper * upper_mean
     up[...] = jnp.concatenate([upper[:own]] * (128 // own), axis=0).T[:SLOT]
     for off in dept_order[:-1]:
         send_up(off).start()
 
-    turn(stores // half - 1)
-    write_base = pltpu.make_async_copy(base, base_out, out_sem.at[0])
-    write_base.start()
 
     packed = lax.broadcasted_iota(jnp.int32, ci.shape, 0) * PACK
     packed_lane = lax.broadcasted_iota(jnp.int32, ci.shape, 1)

time: 32.5 us -> 31 us (0.954)
  Pallas kernels: 31.7 us -> 30.2 us
    pallas_call x1, Pallas kernels: 29.4 us -> 27.9 us  [body(): pl.pallas_call(functools.partial(main_kernel, n_store, n_dept, stores, it...]
where the time goes in v3:
time: 31 us; the launch traced here: 30.8 us
  Pallas kernels  30.2 us (97%)
  between operations  0.64 us (2%)
    pallas_call x1, Pallas kernels, body(): pl.pallas_call(functools.partial(main_kernel, n_store, n_dept, stores, it...  27.9 us
    pallas_call x1, Pallas kernels, body(): pl.pallas_call(functools.partial(final_kernel, items, horizon), out_shape...  2.31 us

profile of v3, /device:TPU:0, one launch (start us, length us, event | category | flops | bytes accessed | tf_op | source)
XLA Modules:
  0.0 30.8 jit_solution(4465819056060944117)
XLA Ops:
  0.6 27.9 %shard_map.67 = (f32[768,256]{1,0:T(8,128)}, f32[72,256]{1,0:T(8,128)}) custom-call(bf16[6144,512]{1,0:T(8,128)(2,1)} %bitcast.4, bf16[512,512]{1,0:T(8,128)(2,1)} %w1_hbm.1, bf16[512,512]{1,0:T(8,128)(2,1)} %w2_hbm.1, bf16[28,512]{1,0:T(8,128)(2,1)} %bitcast.5), custom_call_target="tpu_custom_call" | custom-call | tf_op jit(solution)/shard_map/pallas_call | solution.py:379
  28.5 2.3 %shard_map.68 = (f32[672,256]{1,0:T(8,128)}, f32[28,256]{1,0:T(8,128)}, f32[24,28]{1,0:T(8,128)}) custom-call(f32[768,256]{1,0:T(8,128)} %get-tuple-element.8.base_hbm, f32[72,256]{1,0:T(8,128)} %get-tuple-element.9.small_hbm), custom_call_target="tpu_custom_call" | custom-call | tf_op jit(solution)/shard_map/pallas_call | solution.py:441
